TPU v7x, 512 devices: a whole 4x4x16 slice. The times are simulated.
512 devices in a mesh: blk: 16 (over y, x_hi, core), dom: 32 (over z, x_lo).
Axes of the slice: x: 4 (x_hi: 2, x_lo: 2; x = x_hi * 2 + x_lo), y: 4, z: 16, core: 2. Of those that a mesh axis runs over, the one named last changes fastest.
Arguments:
- hidden_values: bfloat16 [65536, 256], P(('blk', 'dom')), may hold values from -6 to 6
- node_scale: float32 [65536], P(('blk', 'dom')), may hold values from 0.25 to 2
- node_weight: int32 [65536], P(('blk', 'dom')), may hold values from 8 to 24
- weight: bfloat16 [256, 256], replicated, may hold values from -0.375 to 0.375
- cotangent: bfloat16 [65536, 256], P(('blk', 'dom')), may hold values from -6 to 6
- block_rows: int32 [16, 32, 96], P('blk', 'dom'), may hold values from 0 to 31
- block_cols: int32 [16, 32, 96], P('blk', 'dom'), may hold values from 0 to 15
- block_count: int32 [16, 32], P('blk', 'dom'), may hold values from 1 to 96, as said below
- edge_counts: bfloat16 [16, 32, 96, 128, 128], P('blk', 'dom'), may hold values from 0 to 3, as said below
Outputs:
- activated: bfloat16 [65536, 256], P(('blk', 'dom'))
- grad_hidden: bfloat16 [65536, 256], P(('blk', 'dom'))
Inputs may be any that keep to these rules, and one draw needn't show every extreme that they name: The first block_count[b, d] slots of a device hold its blocks and the others are unused; some device uses all 96 slots. `edge_counts`: whole numbers of edges; most entries of a block are zero.
All inputs are finite; a program needn't handle non-finite values.
Results may differ from a plain program's by a relative error of at most 0.028.
Values may be sent and summed in bfloat16 or wider, within the bound.
No kernel may reach another device: no remote copies, remote signals or barrier semaphores. Data moves between devices by JAX's collectives and lax.ppermute only.
A program may use at most 64 MiB of HBM per device.

v0:
```python
import jax
import jax.numpy as jnp
from jax import lax
from jax.sharding import PartitionSpec as P

HID = 256
BSZ = 128
QDEN = 192
slot_group = 16


def add_group(running, offset, edge_local, live_count, pick_index, place_index, source, pattern):
    chosen = lax.dynamic_slice_in_dim(edge_local, offset, slot_group, 0)
    slot_ids = offset + jnp.arange(slot_group, dtype=jnp.int32)
    chosen = jnp.where((slot_ids < live_count)[:, None, None], chosen, jnp.zeros_like(chosen))
    pick_rows = lax.dynamic_slice_in_dim(pick_index, offset, slot_group, 0)
    places = lax.dynamic_slice_in_dim(place_index, offset, slot_group, 0)
    tile_rows = jnp.take(source, pick_rows, axis=0)
    contrib = jnp.einsum(pattern, chosen, tile_rows, preferred_element_type=jnp.float32)
    return running.at[places].add(contrib)


def accumulate(
    running, group_turns, edge_local, live_count, pick_index, place_index, source, pattern
):

    def one_group(group_number, current):
        return add_group(
            current,
            group_number * slot_group,
            edge_local,
            live_count,
            pick_index,
            place_index,
            source,
            pattern,
        )

    return lax.fori_loop(0, group_turns, one_group, running)


def slope_of(preact):
    sigmoid_pre = jax.nn.sigmoid(preact)
    return sigmoid_pre * (1.0 + preact * (1.0 - sigmoid_pre))


def per_device(
    hidden_values,
    node_scale,
    node_weight,
    weight,
    cotangent,
    block_rows,
    block_cols,
    block_count,
    edge_counts,
):
    own_rows = hidden_values.shape[0]
    node_norm = node_weight.astype(jnp.float32) / QDEN
    scaled = (hidden_values.astype(jnp.float32) * (node_scale * node_norm)[:, None]).astype(
        jnp.bfloat16
    )
    gathered = lax.all_gather(scaled, "blk", axis=0, tiled=True)
    column_tiles = gathered.reshape(-1, BSZ, HID)
    edge_local = edge_counts[0, 0]
    rows_local = block_rows[0, 0]
    cols_local = block_cols[0, 0]
    live_count = block_count[0, 0]
    slot_total = edge_local.shape[0]
    group_turns = slot_total // slot_group
    row_blocks = lax.axis_size("dom") * (own_rows // BSZ)
    forward_sums = accumulate(
        jnp.zeros((row_blocks, BSZ, HID), jnp.float32),
        group_turns,
        edge_local,
        live_count,
        cols_local,
        rows_local,
        column_tiles,
        "kji,kjh->kih",
    )
    forward_flat = forward_sums.reshape(row_blocks * BSZ, HID)
    summed = lax.psum_scatter(
        forward_flat.astype(jnp.bfloat16), "dom", scatter_dimension=0, tiled=True
    ).astype(jnp.float32)
    aggregated = (summed * node_norm[:, None]).astype(jnp.bfloat16)
    preact = jnp.dot(aggregated, weight, preferred_element_type=jnp.float32)
    activated = jax.nn.silu(preact).astype(jnp.bfloat16)
    dpre = (cotangent.astype(jnp.float32) * slope_of(preact)).astype(jnp.bfloat16)
    back_own = (
        jnp.dot(dpre, weight.T, preferred_element_type=jnp.float32) * node_norm[:, None]
    ).astype(jnp.bfloat16)
    back_all = lax.all_gather(back_own, "dom", axis=0, tiled=True)
    row_tiles = back_all.reshape(-1, BSZ, HID)
    column_blocks = column_tiles.shape[0]
    backward_sums = accumulate(
        jnp.zeros((column_blocks, BSZ, HID), jnp.float32),
        group_turns,
        edge_local,
        live_count,
        rows_local,
        cols_local,
        row_tiles,
        "kji,kih->kjh",
    )
    column_sums = lax.psum_scatter(
        backward_sums.reshape(column_blocks * BSZ, HID).astype(jnp.bfloat16),
        "blk",
        scatter_dimension=0,
        tiled=True,
    ).astype(jnp.float32)
    grad_hidden = (column_sums * node_norm[:, None]).astype(jnp.bfloat16)
    return (activated, grad_hidden)


def solution(mesh):
    return jax.shard_map(
        per_device,
        mesh=mesh,
        in_specs=(
            P(("blk", "dom"), None),
            P(("blk", "dom")),
            P(("blk", "dom")),
            P(),
            P(("blk", "dom"), None),
            P("blk", "dom", None),
            P("blk", "dom", None),
            P("blk", "dom"),
            P("blk", "dom", None, None, None),
        ),
        out_specs=(P(("blk", "dom"), None), P(("blk", "dom"), None)),
        check_vma=False,
    )
```

profile of v0, /device:TPU:32, one launch (start us, length us, event | category | flops | bytes accessed | tf_op | source)
XLA Modules:
  0.0 574.5 jit_solution(5993749015452363039)
XLA Ops:
  7.9 1.6 multiply_convert_fusion.4
  9.6 66.7 %all-gather.3.cloned.1.call-done = bf16[2048,256]{1,0:T(8,128)(2,1)} async-done(((bf16[128,256]{1,0:T(8,128)(2,1)}), bf16[2048,256]{1,0:T(8,128)(2,1)}) %all-gather.3.cloned.1.call-update) | async-done | bytes 1048592 | tf_op jit(solution)/shard_map/all_gather | solution.py:63
  76.3 2.4 broadcast_in_dim.111
  78.7 64.9 %while.26 = (s32[]{:T(128)}, f32[32,128,256]{2,1,0:T(8,128)}, s32[96]{0:T(128)S(1)}, s32[]{:T(128)}, bf16[96,128,128]{2,1,0:T(8,128)(2,1)}, /*index=5*/s32[96]{0...) while((s32[]{:T(128)}, f32[32,128,256]{2,1,0:T(8,128)}, ...), condition=%wide.region_2.3_spmd, body=%wide.region_0.2_spmd.sunk | while | flops 135529648 | bytes 14160559 | solution.py:39
  79.5 1.8 gather_fusion
  83.4 1.5 fusion.36
  85.1 4.4 scatter_fusion
  90.2 1.8 gather_fusion
  94.2 1.5 fusion.36
  95.8 4.4 scatter_fusion
  100.9 1.8 gather_fusion
  104.9 1.5 fusion.36
  106.5 4.6 scatter_fusion
  111.8 1.8 gather_fusion
  115.8 1.5 fusion.36
  117.5 4.5 scatter_fusion
  122.7 1.8 gather_fusion
  126.7 1.5 fusion.36
  128.3 4.5 scatter_fusion
  133.6 1.8 gather_fusion
  139.2 4.4 scatter_fusion
  143.6 3.8 convert_element_type.48
  147.5 135.7 %reduce-scatter.3.cloned.1.call-done = bf16[128,256]{1,0:T(8,128)(2,1)} async-done(((bf16[4096,256]{1,0:T(8,128)(2,1)}), bf16[128,256]{1,0:T(8,128)(2,1)}) %reduce-scatter.3.cloned.1.call-update) | async-done | bytes 65552 | tf_op jit(solution)/shard_map/reduce_scatter | solution.py:83
  283.2 1.7 multiply_convert_fusion.2
  285.8 132.6 %all-gather.5.cloned.1.call-done = bf16[4096,256]{1,0:T(8,128)(2,1)} async-done(((bf16[128,256]{1,0:T(8,128)(2,1)}), bf16[4096,256]{1,0:T(8,128)(2,1)}) %all-gather.5.cloned.1.call-update) | async-done | bytes 2097168 | tf_op jit(solution)/shard_map/all_gather | solution.py:93
  418.4 1.5 broadcast_in_dim.112
  419.9 53.5 %while.27 = (s32[]{:T(128)}, f32[16,128,256]{2,1,0:T(8,128)}, s32[96]{0:T(128)S(1)}, s32[]{:T(128)}, bf16[96,128,128]{2,1,0:T(8,128)(2,1)}, /*index=5*/s32[96]{0...) while((s32[]{:T(128)}, f32[16,128,256]{2,1,0:T(8,128)}, ...), condition=%wide.region_6.7_spmd, body=%wide.region_4.6_spmd.sunk | while | flops 135529648 | bytes 12063407 | solution.py:39
  420.7 2.2 gather_fusion.1
  422.9 1.5 fusion.39
  424.5 4.3 scatter_fusion.1
  429.6 2.2 gather_fusion.1
  431.8 1.5 fusion.39
  433.4 4.3 scatter_fusion.1
  438.5 2.2 gather_fusion.1
  440.7 1.5 fusion.39
  442.3 4.4 scatter_fusion.1
  447.4 2.2 gather_fusion.1
  449.6 1.5 fusion.39
  451.3 4.4 scatter_fusion.1
  456.4 2.2 gather_fusion.1
  458.6 1.5 fusion.39
  460.2 4.3 scatter_fusion.1
  465.3 2.2 gather_fusion.1
  467.5 1.5 fusion.39
  469.1 4.4 scatter_fusion.1
  473.5 2.7 convert_element_type.56
  476.2 90.2 %reduce-scatter.5.cloned.1.call-done = bf16[128,256]{1,0:T(8,128)(2,1)} async-done(((bf16[2048,256]{1,0:T(8,128)(2,1)}), bf16[128,256]{1,0:T(8,128)(2,1)}) %reduce-scatter.5.cloned.1.call-update) | async-done | bytes 65552 | tf_op jit(solution)/shard_map/reduce_scatter | solution.py:106
  566.4 1.6 multiply_convert_fusion
  (67 shorter events, 25.9 us)
Async XLA Ops:
  7.2 276.0 %copy-start = (bf16[256,256]{1,0:T(8,128)(2,1)S(1)}, bf16[256,256]{1,0:T(8,128)(2,1)}, u32[]{:S(2)}) copy-start(bf16[256,256]{1,0:T(8,128)(2,1)} %param.16) | copy-start | bytes 393220
  7.2 69.1 %all-gather.3.cloned.1.call-start = ((), (), s32[]{:S(2)}) async-start(), calls=%async_computation.2 | async-start | bytes 1114112 | tf_op jit(solution)/shard_map/all_gather | solution.py:63
  9.5 273.7 %reduce-scatter.3.cloned.1.call-start = ((), (), s32[]{:S(2)}) async-start(), calls=%async_computation.3 | async-start | bytes 2162688 | tf_op jit(solution)/shard_map/reduce_scatter | solution.py:83
  76.3 2.4 copy-start.1
  76.3 2.4 copy-start.2
  147.5 137.5 %copy-start.3 = (bf16[128,256]{1,0:T(8,128)(2,1)S(1)}, bf16[128,256]{1,0:T(8,128)(2,1)}, u32[]{:S(2)}) copy-start(bf16[128,256]{1,0:T(8,128)(2,1)} %param.17) | copy-start | bytes 196612
  147.5 270.9 %all-gather.5.cloned.1.call-start = ((), (), s32[]{:S(2)}) async-start(), calls=%async_computation.4 | async-start | bytes 2162688 | tf_op jit(solution)/shard_map/all_gather | solution.py:93
  285.8 280.7 %reduce-scatter.5.cloned.1.call-start = ((), (), s32[]{:S(2)}) async-start(), calls=%async_computation.5 | async-start | bytes 1114112 | tf_op jit(solution)/shard_map/reduce_scatter | solution.py:106
Sparse Core Ops, SparseCore 0:
  11.9 64.2 all-gather.2
  147.6 135.5 reduce-scatter.2
  286.1 132.2 all-gather.4
  476.3 90.0 reduce-scatter.4
where the time goes:
time: 577 us; the launch traced here: 575 us
  waiting for transfers between devices  425 us (74%)
  other arithmetic  73 us (13%)
  local copies, waits for them, and re-layouts  41.1 us (7%)
  matrix products  21 us (4%)
  between operations  13.8 us (2%)
    reduce_scatter x1, waiting for transfers between devices, per_device(): lax.psum_scatter(forward_flat.astype(jnp.bfloat16), 'dom', scatter_dimens...  136 us
    all_gather x1, waiting for transfers between devices, per_device(): back_all = lax.all_gather(back_own, 'dom', axis=0, tiled=True)  133 us
    reduce_scatter x1, waiting for transfers between devices, per_device(): lax.psum_scatter(backward_sums.reshape(column_blocks * BSZ, HID).astype(j...  90.2 us
    all_gather x1, waiting for transfers between devices, per_device(): gathered = lax.all_gather(scaled, 'blk', axis=0, tiled=True)  66.7 us
    scatter-add x12, other arithmetic, add_group(): return running.at[places].add(contrib)  52.9 us
    gather x12, local copies, waits for them, and re-layouts, add_group(): tile_rows = jnp.take(source, pick_rows, axis=0)  24.3 us
    dot_general x12, matrix products, add_group(): jnp.einsum(pattern, chosen, tile_rows, preferred_element_type=jnp.float32)  18.5 us
    dynamic_slice x12, local copies, waits for them, and re-layouts, add_group(): chosen = lax.dynamic_slice_in_dim(edge_local, offset, slot_group, 0)  12.8 us
  transfers between devices with their start and end apart: 4, of which 4 were waited for; matrix products, arithmetic and copies ran while one was open for 0% of the time, Pallas kernels for 0%

commit v1 on v0

--- a/solution.py
+++ b/solution.py
@@ -60,7 +60,9 @@
     scaled = (hidden_values.astype(jnp.float32) * (node_scale * node_norm)[:, None]).astype(
         jnp.bfloat16
     )
-    gathered = lax.all_gather(scaled, "blk", axis=0, tiled=True)
+    gathered = jnp.concatenate(
+        lax.all_to_all(jnp.stack([scaled] * lax.axis_size("blk")), "blk", 0, 0), axis=0
+    )
     column_tiles = gathered.reshape(-1, BSZ, HID)
     edge_local = edge_counts[0, 0]
     rows_local = block_rows[0, 0]

time: 577 us -> 536 us (0.929)
  waiting for transfers between devices: 425 us -> 377 us
  starting transfers between devices: 0.16 us -> 7.21 us
    all_gather x1 -> x0, waiting for transfers between devices: 66.7 us -> none  [per_device(): gathered = lax.all_gather(scaled, 'blk', axis=0, tiled=True)]
    all_to_all x0 -> x1, waiting for transfers between devices: none -> 18 us  [per_device(): lax.all_to_all(jnp.stack([scaled] * lax.axis_size('blk')), 'blk', 0, 0)]
    all_to_all x0 -> x1, starting transfers between devices: none -> 7.09 us  [per_device(): lax.all_to_all(jnp.stack([scaled] * lax.axis_size('blk')), 'blk', 0, 0)]
where the time goes in v1:
time: 536 us; the launch traced here: 534 us
  waiting for transfers between devices  377 us (70%)
  other arithmetic  72.2 us (13%)
  local copies, waits for them, and re-layouts  42 us (8%)
  matrix products  21 us (4%)
  between operations  13.8 us (3%)
  starting transfers between devices  7.21 us (1%)
    reduce_scatter x1, waiting for transfers between devices, per_device(): lax.psum_scatter(forward_flat.astype(jnp.bfloat16), 'dom', scatter_dimens...  136 us
    all_gather x1, waiting for transfers between devices, per_device(): back_all = lax.all_gather(back_own, 'dom', axis=0, tiled=True)  133 us
    reduce_scatter x1, waiting for transfers between devices, per_device(): lax.psum_scatter(backward_sums.reshape(column_blocks * BSZ, HID).astype(j...  90.3 us
    scatter-add x12, other arithmetic, add_group(): return running.at[places].add(contrib)  52.8 us
    gather x12, local copies, waits for them, and re-layouts, add_group(): tile_rows = jnp.take(source, pick_rows, axis=0)  24.3 us
    dot_general x12, matrix products, add_group(): jnp.einsum(pattern, chosen, tile_rows, preferred_element_type=jnp.float32)  18.5 us
    all_to_all x1, waiting for transfers between devices, per_device(): lax.all_to_all(jnp.stack([scaled] * lax.axis_size('blk')), 'blk', 0, 0)  18 us
    dynamic_slice x12, local copies, waits for them, and re-layouts, add_group(): chosen = lax.dynamic_slice_in_dim(edge_local, offset, slot_group, 0)  12.7 us
  transfers between devices with their start and end apart: 4, of which 4 were waited for; matrix products, arithmetic and copies ran while one was open for 0% of the time, Pallas kernels for 0%

profile of v1, /device:TPU:32, one launch (start us, length us, event | category | flops | bytes accessed | tf_op | source)
XLA Modules:
  0.0 533.8 jit_solution(3634788665941681921)
XLA Ops:
  9.9 7.1 %all-to-all-start = ((bf16[16,128,256]{2,1,0:T(8,128)(2,1)}), bf16[16,128,256]{2,1,0:T(8,128)(2,1)}, u32[]{:S(2)}, u32[]{:S(2)}) async-start(bf16[16,128,256]{2,1,0:T(8,128)(2,1)} %stack.2), calls=%async_computation | async-start | bytes 2097152 | tf_op jit(solution)/shard_map/all_to_all | solution.py:64
  17.0 18.0 %all-to-all-done = bf16[16,128,256]{2,1,0:T(8,128)(2,1)} async-done(((bf16[16,128,256]{2,1,0:T(8,128)(2,1)}), bf16[16,128,256]{2,1,0:T(8,128)(2,1)}, u32[]{:S(2)}, u32[]{:S(2)}) %all-to-all-start) | async-done | bytes 1048608 | tf_op jit(solution)/shard_map/all_to_all | solution.py:64
  35.1 2.4 broadcast_in_dim.111
  37.5 64.7 %while.26 = (s32[]{:T(128)}, f32[32,128,256]{2,1,0:T(8,128)}, s32[96]{0:T(128)S(1)}, s32[]{:T(128)}, bf16[96,128,128]{2,1,0:T(8,128)(2,1)}, /*index=5*/s32[96]{0...) while((s32[]{:T(128)}, f32[32,128,256]{2,1,0:T(8,128)}, ...), condition=%wide.region_2.3_spmd, body=%wide.region_0.2_spmd.sunk | while | flops 135529648 | bytes 14160559 | solution.py:39
  38.2 1.8 gather_fusion
  42.2 1.5 fusion.36
  43.8 4.4 scatter_fusion
  48.9 1.8 gather_fusion
  52.9 1.5 fusion.36
  54.5 4.4 scatter_fusion
  59.7 1.8 gather_fusion
  63.6 1.5 fusion.36
  65.2 4.5 scatter_fusion
  70.5 1.8 gather_fusion
  74.5 1.5 fusion.36
  76.1 4.5 scatter_fusion
  81.4 1.8 gather_fusion
  85.3 1.5 fusion.36
  87.0 4.5 scatter_fusion
  92.2 1.8 gather_fusion
  97.8 4.4 scatter_fusion
  102.2 3.8 convert_element_type.48
  106.1 135.9 %reduce-scatter.3.cloned.1.call-done = bf16[128,256]{1,0:T(8,128)(2,1)} async-done(((bf16[4096,256]{1,0:T(8,128)(2,1)}), bf16[128,256]{1,0:T(8,128)(2,1)}) %reduce-scatter.3.cloned.1.call-update) | async-done | bytes 65552 | tf_op jit(solution)/shard_map/reduce_scatter | solution.py:85
  242.0 1.7 multiply_convert_fusion.2
  244.7 132.9 %all-gather.2.cloned.1.call-done = bf16[4096,256]{1,0:T(8,128)(2,1)} async-done(((bf16[128,256]{1,0:T(8,128)(2,1)}), bf16[4096,256]{1,0:T(8,128)(2,1)}) %all-gather.2.cloned.1.call-update) | async-done | bytes 2097168 | tf_op jit(solution)/shard_map/all_gather | solution.py:95
  377.6 1.5 broadcast_in_dim.112
  379.1 53.5 %while.27 = (s32[]{:T(128)}, f32[16,128,256]{2,1,0:T(8,128)}, s32[96]{0:T(128)S(1)}, s32[]{:T(128)}, bf16[96,128,128]{2,1,0:T(8,128)(2,1)}, /*index=5*/s32[96]{0...) while((s32[]{:T(128)}, f32[16,128,256]{2,1,0:T(8,128)}, ...), condition=%wide.region_6.7_spmd, body=%wide.region_4.6_spmd.sunk | while | flops 135529648 | bytes 12063407 | solution.py:39
  379.9 2.2 gather_fusion.1
  382.1 1.5 fusion.39
  383.7 4.3 scatter_fusion.1
  388.8 2.2 gather_fusion.1
  391.0 1.5 fusion.39
  392.6 4.3 scatter_fusion.1
  397.6 2.2 gather_fusion.1
  399.9 1.5 fusion.39
  401.5 4.4 scatter_fusion.1
  406.6 2.2 gather_fusion.1
  408.8 1.5 fusion.39
  410.4 4.4 scatter_fusion.1
  415.5 2.2 gather_fusion.1
  417.7 1.5 fusion.39
  419.4 4.3 scatter_fusion.1
  424.4 2.2 gather_fusion.1
  426.7 1.5 fusion.39
  428.3 4.4 scatter_fusion.1
  432.6 2.7 convert_element_type.56
  435.4 90.3 %reduce-scatter.5.cloned.1.call-done = bf16[128,256]{1,0:T(8,128)(2,1)} async-done(((bf16[2048,256]{1,0:T(8,128)(2,1)}), bf16[128,256]{1,0:T(8,128)(2,1)}) %reduce-scatter.5.cloned.1.call-update) | async-done | bytes 65552 | tf_op jit(solution)/shard_map/reduce_scatter | solution.py:108
  525.7 1.6 multiply_convert_fusion
  (67 shorter events, 27.7 us)
Async XLA Ops:
  7.2 234.9 %copy-start = (bf16[256,256]{1,0:T(8,128)(2,1)S(1)}, bf16[256,256]{1,0:T(8,128)(2,1)}, u32[]{:S(2)}) copy-start(bf16[256,256]{1,0:T(8,128)(2,1)} %param.16) | copy-start | bytes 393220
  9.9 25.2 %all-to-all-start = ((bf16[16,128,256]{2,1,0:T(8,128)(2,1)}), bf16[16,128,256]{2,1,0:T(8,128)(2,1)}, u32[]{:S(2)}, u32[]{:S(2)}) async-start(bf16[16,128,256]{2,1,0:T(8,128)(2,1)} %stack.2), calls=%async_computation | async-start | bytes 2097152 | tf_op jit(solution)/shard_map/all_to_all | solution.py:64
  17.0 225.0 %reduce-scatter.3.cloned.1.call-start = ((), (), s32[]{:S(2)}) async-start(), calls=%async_computation.3 | async-start | bytes 2162688 | tf_op jit(solution)/shard_map/reduce_scatter | solution.py:85
  35.1 2.4 copy-start.1
  35.1 2.4 copy-start.2
  106.0 137.7 %copy-start.3 = (bf16[128,256]{1,0:T(8,128)(2,1)S(1)}, bf16[128,256]{1,0:T(8,128)(2,1)}, u32[]{:S(2)}) copy-start(bf16[128,256]{1,0:T(8,128)(2,1)} %param.17) | copy-start | bytes 196612
  106.1 271.5 %all-gather.2.cloned.1.call-start = ((), (), s32[]{:S(2)}) async-start(), calls=%async_computation.4 | async-start | bytes 2162688 | tf_op jit(solution)/shard_map/all_gather | solution.py:95
  244.6 281.1 %reduce-scatter.5.cloned.1.call-start = ((), (), s32[]{:S(2)}) async-start(), calls=%async_computation.5 | async-start | bytes 1114112 | tf_op jit(solution)/shard_map/reduce_scatter | solution.py:108
Sparse Core Ops, SparseCore 0:
  106.2 135.8 reduce-scatter.2
  244.9 132.6 all-gather.1
  435.5 90.1 reduce-scatter.4
